TPU v7x, 32 devices: a whole 2x2x4 slice. The times are simulated.
32 devices in a mesh: groups: 2 (over y), gx: 4 (over x, core), vert: 4 (over z).
Axes of the slice: x: 2, y: 2, z: 4, core: 2. Of those that a mesh axis runs over, the one named last changes fastest.
Arguments:
- distribution: float32 [64, 16, 16, 2048], P(('groups', 'gx'), None, None, 'vert'), parts along dimension 0, may hold values from 0.05 to 2
- velocity_order: int32 [2048], P('vert'), may hold values from 0 to 2047, each once
- cell_codes: int32 [64, 16, 16], P(('groups', 'gx')), parts along dimension 0, may hold values from 0 to 2, as said below
- knudsen: float32 [2], P('groups'), parts along dimension 0, may hold values from 0.05 to 1
- inflow: float32 [8], P('groups'), parts along dimension 0, may hold values from 0.5 to 1.5
Outputs:
- evolved: float32 [64, 16, 16, 2048], P(('groups', 'gx'), None, None, 'vert'), parts along dimension 0
There are 2 independent parts, one for each index of `groups`. A program takes and returns all parts, laid end to end along the dimension named above; an argument that names none is the same for every part. Nothing has to cross between parts.
Inputs may be any that keep to these rules, and one draw needn't show every extreme that they name: `velocity_order`: names each of the 2048 velocity grid points once. `cell_codes`: 0 marks an open cell, 1 an inflow cell, 2 a wall cell.
All inputs are finite; a program needn't handle non-finite values.
Results may differ from a plain program's by a relative error of at most 0.0003.
Values sent between devices are 32-bit elements; how exact they have to be, the bound alone decides.
A program may use at most 128 MiB of HBM per device.

v0:
```python
import functools

import jax
import jax.numpy as jnp
from jax import lax
from jax.experimental import pallas as pl
from jax.experimental.pallas import tpu as pltpu
from jax.sharding import PartitionSpec as P

VGX = 16
VGY = 16
VGZ = 8
STEPS = 3
LANES = 128
LOG2E = 1.4426950408889634
MESH = pl.DeviceIdType.MESH

H1 = 3.0 / VGX
H2 = 3.0 / VGY
H3 = 3.0 / VGZ


def minmod(lower, upper):
    return jnp.maximum(jnp.minimum(lower, upper), 0.0) + jnp.minimum(
        jnp.maximum(lower, upper), 0.0
    )


def split3(value):
    high = value.astype(jnp.bfloat16).astype(jnp.float32)
    rest = value - high
    middle = rest.astype(jnp.bfloat16).astype(jnp.float32)
    return high, middle, rest - middle


def kernel(
    rows, ny, nz, width, nx_dev, nv,
    dist, order, codes, knudsen, inflow,
    out,
    state, moved, halo_low, halo_high, mom, coef, feat, wide, cour,
    in_sem, out_sem, halo_send, halo_recv, mom_send, mom_recv,
):
    cells = ny * nz
    tiles = width // LANES
    total = float(width * nv)
    half = rows // 2
    group_cells = half * cells
    mx = lax.axis_index("gx")
    mv = lax.axis_index("vert")
    has_low = mx > 0
    has_high = mx < nx_dev - 1

    load = pltpu.make_async_copy(dist, state, in_sem)
    load.start()

    barrier = pltpu.get_barrier_semaphore()

    @pl.when(has_low)
    def _():
        pl.semaphore_signal(barrier, inc=1, device_id={"gx": mx - 1}, device_id_type=MESH)

    @pl.when(has_high)
    def _():
        pl.semaphore_signal(barrier, inc=1, device_id={"gx": mx + 1}, device_id_type=MESH)

    for p in range(1, nv):
        pl.semaphore_signal(
            barrier, inc=1, device_id={"vert": lax.rem(mv + p, nv)}, device_id_type=MESH
        )
    pl.semaphore_wait(
        barrier, nv - 1 + has_low.astype(jnp.int32) + has_high.astype(jnp.int32)
    )

    def to_low(t, source):
        return pltpu.make_async_remote_copy(
            src_ref=source.at[pl.ds(0, 2)],
            dst_ref=halo_high.at[t],
            send_sem=halo_send.at[t, 0],
            recv_sem=halo_recv.at[t, 0],
            device_id={"gx": mx - 1},
            device_id_type=MESH,
        )

    def to_high(t, source):
        return pltpu.make_async_remote_copy(
            src_ref=source.at[pl.ds(rows - 2, 2)],
            dst_ref=halo_low.at[t],
            send_sem=halo_send.at[t, 1],
            recv_sem=halo_recv.at[t, 1],
            device_id={"gx": mx + 1},
            device_id_type=MESH,
        )

    @pl.when(has_low)
    def _():
        to_low(0, dist).start()

    @pl.when(has_high)
    def _():
        to_high(0, dist).start()

    slot = order[...]
    odd1 = (2 * (slot // (VGY * VGZ)) + 1 - VGX).astype(jnp.float32)
    odd2 = (2 * ((slot // VGZ) % VGY) + 1 - VGY).astype(jnp.float32)
    odd3 = (2 * (slot % VGZ) + 1 - VGZ).astype(jnp.float32)
    ratio = (H3 / H1) ** 2
    table = jnp.concatenate(
        [
            jnp.ones_like(odd1), odd1, odd2, odd3,
            odd1 * odd1, odd2 * odd2, ratio * odd3 * odd3, jnp.zeros_like(odd1),
        ],
        axis=0,
    )
    feat[...] = jnp.concatenate([table, jnp.zeros_like(table)], axis=0).astype(jnp.bfloat16)
    keep_row = (lax.broadcasted_iota(jnp.int32, (8, LANES), 0) == 7).astype(jnp.float32)
    broad = jnp.concatenate([table, keep_row], axis=1)
    wide[...] = jnp.concatenate([broad, broad, broad, jnp.zeros_like(broad)], axis=0).astype(
        jnp.bfloat16
    )
    speeds = []
    for speed in (0.1 * H1 * odd1, (H2 / 30.0) * odd2, (H3 / 30.0) * odd3):
        gain = 0.5 * (1.0 - jnp.abs(speed)) * jnp.where(speed > 0, 1.0, -1.0)
        speeds += [speed, gain]
    cour[...] = jnp.concatenate(speeds + [jnp.zeros_like(odd1)] * 2, axis=0)

    @pl.when(jnp.logical_not(has_low))
    def _():
        halo_low[...] = jnp.zeros_like(halo_low)

    @pl.when(jnp.logical_not(has_high))
    def _():
        halo_high[...] = jnp.zeros_like(halo_high)

    load.wait()

    def constants(j, dim):
        lanes = pl.ds(pl.multiple_of(j * LANES, LANES), LANES)
        speed = jnp.broadcast_to(cour[2 * dim:2 * dim + 1, lanes], (nz, LANES))
        gain = jnp.broadcast_to(cour[2 * dim + 1:2 * dim + 2, lanes], (nz, LANES))
        return lanes, speed, gain, speed > 0

    def yz_tile(index, _):
        x = index // tiles
        lanes, speed2, gain2, ahead2 = constants(index % tiles, 1)
        _, speed3, gain3, ahead3 = constants(index % tiles, 2)

        def cell(y):
            return state[x, y % ny, :, lanes]

        f_low = cell(-2)
        f_mid = cell(-1)
        f = cell(0)
        d_low = f_mid - f_low
        d = f - f_mid
        l_low = f_mid + gain2 * minmod(d_low, d)
        f_up = cell(1)
        d_up = f_up - f
        l = f + gain2 * minmod(d, d_up)
        change = l - l_low
        for y in range(ny):
            f_next = cell(y + 2)
            d_next = f_next - f_up
            l_up = f_up + gain2 * minmod(d_up, d_next)
            change_up = l_up - l
            result = f - speed2 * jnp.where(ahead2, change, change_up)
            dz = pltpu.roll(f, nz - 1, 0) - f
            lz = f + gain3 * minmod(pltpu.roll(dz, 1, 0), dz)
            face = jnp.where(ahead3, lz, pltpu.roll(lz, nz - 1, 0))
            moved[x, y, :, lanes] = result - speed3 * (face - pltpu.roll(face, 1, 0))
            f, f_up = f_up, f_next
            d_up = d_next
            l, change = l_up, change_up
        return 0

    YU = 4

    def x_tile(t, sources, outputs, index, _):
        lanes, speed, gain, ahead = constants(index % tiles, 0)
        for k in range(YU):
            y = (index // tiles) * YU + k
            f = [ref[(*lead, y, slice(None), lanes)] for ref, lead in sources]
            d = [b - a for a, b in zip(f[:-1], f[1:])]
            l = [f[i + 1] + gain * minmod(d[i], d[i + 1]) for i in range(len(d) - 1)]
            c = [b - a for a, b in zip(l[:-1], l[1:])]
            for i, x in enumerate(outputs):
                moved[x, y, :, lanes] = moved[x, y, :, lanes] - speed * jnp.where(
                    ahead, c[i], c[i + 1]
                )
        return 0

    def layer_of(group, i):
        return i + 2 if group == 1 else i + half * (i // 2)

    def moments(t, group):
        def layer(i, _):
            x = layer_of(group, i)
            flat = moved[x].reshape(cells, width)
            high = flat.astype(jnp.bfloat16)
            low = (flat - high.astype(jnp.float32)).astype(jnp.bfloat16)
            sums = lax.dot_general(
                feat[...], high, (((1,), (1,)), ((), ())), preferred_element_type=jnp.float32
            ) + lax.dot_general(
                feat[...], low, (((1,), (1,)), ((), ())), preferred_element_type=jnp.float32
            )
            mom[t, group, mv, i] = sums[0:8]
            return 0

        lax.fori_loop(0, half, layer, 0)

    def mom_copy(t, group, p):
        return pltpu.make_async_remote_copy(
            src_ref=mom.at[t, group, mv],
            dst_ref=mom.at[t, group, mv],
            send_sem=mom_send.at[t, group, p - 1],
            recv_sem=mom_recv.at[t, group, p - 1],
            device_id={"vert": lax.rem(mv + p, nv)},
            device_id_type=MESH,
        )

    def send_moments(t, group):
        for p in range(1, nv):
            mom_copy(t, group, p).start()

    def coefficients(t, group):
        for p in range(1, nv):
            mom_copy(t, group, p).wait_recv()
        sums = []
        for i in range(half):
            layer = mom[t, group, 0, i]
            for v in range(1, nv):
                layer = layer + mom[t, group, v, i]
            sums.append(layer)
        sums = jnp.concatenate(sums, axis=1)
        weight = sums[0:1]
        density = weight / total
        inverse = 1.0 / weight
        u1 = H1 * sums[1:2] * inverse
        u2 = H2 * sums[2:3] * inverse
        u3 = H3 * sums[3:4] * inverse
        square = (H1 * H1) * (sums[4:5] + sums[5:6] + sums[6:7]) * inverse
        temperature = (square - (u1 * u1 + u2 * u2 + u3 * u3)) / 3.0
        code = codes[group]
        is_inflow = code == 1
        is_wall = code == 2
        is_open = jnp.logical_not(jnp.logical_or(is_inflow, is_wall))
        rate = 0.5 * density / (density + knudsen[0])
        zero = jnp.zeros_like(u1)
        u1 = jnp.where(is_inflow, inflow[1], jnp.where(is_wall, zero, u1))
        u2 = jnp.where(is_open, u2, zero)
        u3 = jnp.where(is_open, u3, zero)
        temperature = jnp.where(
            is_inflow, inflow[2], jnp.where(is_wall, inflow[3], temperature)
        )
        front = jnp.where(is_inflow, inflow[0], jnp.where(is_wall, density, rate * density))
        keep = jnp.where(is_open, 1.0 - rate, zero)
        sharp = (0.5 * LOG2E) / temperature

        def axis_sum(count, step, u):
            grid = lax.broadcasted_iota(jnp.int32, (count, group_cells), 0).astype(jnp.float32)
            away = (2.0 * grid + (1.0 - count)) * step - u
            return jnp.sum(jnp.exp2(-(away * away) * sharp), axis=0, keepdims=True)

        norm = axis_sum(VGX, H1, u1) * axis_sum(VGY, H2, u2) * axis_sum(VGZ, H3, u3)
        constant = jnp.log2(front * total / norm) - (u1 * u1 + u2 * u2 + u3 * u3) * sharp
        slope = 2.0 * sharp
        quad = -(H1 * H1) * sharp
        packed = jnp.concatenate(
            [
                constant, slope * u1 * H1, slope * u2 * H2, slope * u3 * H3,
                quad, quad, quad, keep,
            ],
            axis=0,
        )
        stacked = jnp.concatenate([*split3(packed), jnp.zeros_like(packed)], axis=0)
        for k in range(group_cells // LANES):
            coef[group, k] = stacked[:, k * LANES:(k + 1) * LANES].T.astype(jnp.bfloat16)

    blocks = cells // LANES
    yb = ny // blocks

    def relax(group, first, count):
        def block(k, _):
            x = layer_of(group, k // blocks)
            ys = pl.ds((k % blocks) * yb, yb)
            power = jnp.dot(coef[group, k], wide[...], preferred_element_type=jnp.float32)
            keep = power[:, width:]
            for j in range(tiles):
                lanes = slice(j * LANES, (j + 1) * LANES)
                old = moved[x, ys, :, lanes].reshape(LANES, LANES)
                new = keep * old + jnp.exp2(power[:, lanes])
                state[x, ys, :, lanes] = new.reshape(yb, nz, LANES)
            return 0

        lax.fori_loop(first * blocks, (first + count) * blocks, block, 0)

    def write_out(first):
        return pltpu.make_async_copy(
            state.at[pl.ds(first, 2)], out.at[pl.ds(first, 2)], out_sem.at[first // 2]
        )

    def step(t, _):
        last = t == STEPS - 1
        lax.fori_loop(0, rows * tiles, yz_tile, 0)
        count = (ny // YU) * tiles
        inner = [(state, (x,)) for x in range(rows)]
        lax.fori_loop(
            0, count, functools.partial(x_tile, t, inner, range(2, rows - 2)), 0
        )
        moments(t, 1)
        send_moments(t, 1)

        @pl.when(has_high)
        def _():
            to_low(t, state).wait_recv()

        @pl.when(has_low)
        def _():
            to_high(t, state).wait_recv()

        low = [(halo_low, (t, 0)), (halo_low, (t, 1))] + inner[:4]
        lax.fori_loop(0, count, functools.partial(x_tile, t, low, (0, 1)), 0)
        high = inner[-4:] + [(halo_high, (t, 0)), (halo_high, (t, 1))]
        lax.fori_loop(
            0, count, functools.partial(x_tile, t, high, (rows - 2, rows - 1)), 0
        )
        moments(t, 0)
        send_moments(t, 0)

        coefficients(t, 1)
        relax(1, 0, half)

        @pl.when(last)
        def _():
            for first in range(2, rows - 2, 2):
                write_out(first).start()

        @pl.when(has_low)
        def _():
            to_low(t, state).wait_send()

        @pl.when(has_high)
        def _():
            to_high(t, state).wait_send()

        coefficients(t, 0)
        relax(0, 0, 2)

        @pl.when(jnp.logical_and(has_low, jnp.logical_not(last)))
        def _():
            to_low(t + 1, state).start()

        relax(0, 2, 2)

        @pl.when(jnp.logical_and(has_high, jnp.logical_not(last)))
        def _():
            to_high(t + 1, state).start()

        for group in range(2):
            for p in range(1, nv):
                mom_copy(t, group, p).wait_send()
        return 0

    lax.fori_loop(0, STEPS, step, 0)
    write_out(0).start()
    write_out(rows - 2).start()
    for first in range(0, rows, 2):
        write_out(first).wait()


def body(distribution, velocity_order, cell_codes, knudsen, inflow):
    rows, ny, nz, width = distribution.shape
    nv = lax.axis_size("vert")
    nx_dev = lax.axis_size("gx")
    cells = ny * nz
    half = rows // 2
    flat = cell_codes.reshape(rows, cells)
    codes = jnp.stack(
        [
            jnp.concatenate([flat[:2], flat[-2:]]).reshape(1, -1),
            flat[2:-2].reshape(1, -1),
        ]
    )
    vmem = pl.BlockSpec(memory_space=pltpu.VMEM)
    smem = pl.BlockSpec(memory_space=pltpu.SMEM)
    hbm = pl.BlockSpec(memory_space=pl.ANY)
    return pl.pallas_call(
        functools.partial(kernel, rows, ny, nz, width, nx_dev, nv),
        out_shape=jax.ShapeDtypeStruct(distribution.shape, jnp.float32),
        in_specs=[hbm, vmem, vmem, smem, smem],
        out_specs=hbm,
        scratch_shapes=[
            pltpu.VMEM((rows, ny, nz, width), jnp.float32),
            pltpu.VMEM((rows, ny, nz, width), jnp.float32),
            pltpu.VMEM((STEPS, 2, ny, nz, width), jnp.float32),
            pltpu.VMEM((STEPS, 2, ny, nz, width), jnp.float32),
            pltpu.VMEM((STEPS, 2, nv, half, 8, cells), jnp.float32),
            pltpu.VMEM((2, half * cells // LANES, LANES, 32), jnp.bfloat16),
            pltpu.VMEM((16, width), jnp.bfloat16),
            pltpu.VMEM((32, width + LANES), jnp.bfloat16),
            pltpu.VMEM((8, width), jnp.float32),
            pltpu.SemaphoreType.DMA,
            pltpu.SemaphoreType.DMA((rows // 2,)),
            pltpu.SemaphoreType.DMA((STEPS, 2)),
            pltpu.SemaphoreType.DMA((STEPS, 2)),
            pltpu.SemaphoreType.DMA((STEPS, 2, nv - 1)),
            pltpu.SemaphoreType.DMA((STEPS, 2, nv - 1)),
        ],
        compiler_params=pltpu.CompilerParams(
            collective_id=0, has_side_effects=True, vmem_limit_bytes=48 * 1024 * 1024
        ),
    )(distribution, velocity_order.reshape(1, width), codes, knudsen, inflow)


def solution(mesh):
    placed = (
        P(("groups", "gx"), None, None, "vert"),
        P("vert"),
        P(("groups", "gx"), None, None),
        P("groups"),
        P("groups"),
    )
    return jax.shard_map(
        body,
        mesh=mesh,
        in_specs=placed,
        out_specs=P(("groups", "gx"), None, None, "vert"),
        check_vma=False,
    )
```

profile of v0, /device:TPU:1, one launch (start us, length us, event | category | flops | bytes accessed | tf_op | source)
XLA Modules:
  0.0 76.8 jit_solution(5323557699665116213)
XLA Ops:
  0.7 0.8 slice.20
  1.4 0.1 stack_reshape.7
  1.5 0.7 fusion
  2.2 0.1 slice.17
  2.3 0.1 slice.19
  2.4 0.0 copy-start
  2.5 0.7 copy-done
  3.1 0.0 copy-start.1
  3.1 0.7 copy-done.1
  3.8 71.0 %shard_map.55 = f32[8,16,16,512]{3,2,1,0:T(8,128)S(1)} custom-call(f32[8,16,16,512]{3,2,1,0:T(8,128)} %dist.1, s32[1,512]{1,0:T(1,128)S(1)} %bitcast.1, s32[2,1,1024]{2,1,0:T(1,128)S(1)} %pad_add_fusion.codes, f32[1]{0:T(128)S(6)} %copy.7.knudsen, f32[4]{0:T(128)S(1)} %copy-done.1), custom_call_target="tpu_custom_call" | custom-call | tf_op jit(solution)/shard_map/pallas_call | solution.py:386
  74.8 2.0 %copy.8 = f32[8,16,16,512]{3,2,1,0:T(8,128)} copy(f32[8,16,16,512]{3,2,1,0:T(8,128)S(1)} %shard_map.55) | data formatting | bytes 8388608
  (3 shorter events, 0.0 us)
Async XLA Ops:
  2.4 0.7 copy-start
  3.1 0.7 copy-start.1
where the time goes:
time: 77.1 us; the launch traced here: 76.8 us
  Pallas kernels  71 us (92%)
  local copies, waits for them, and re-layouts  5.12 us (7%)
    pallas_call x1, Pallas kernels, body(): pl.pallas_call(functools.partial(kernel, rows, ny, nz, width, nx_dev, nv)...  71 us
    unnamed x5, local copies, waits for them, and re-layouts  3.35 us

commit v1 on v0

v1 whole, which is shorter than its diff:
```python
import functools

import jax
import jax.numpy as jnp
from jax import lax
from jax.experimental import pallas as pl
from jax.experimental.pallas import tpu as pltpu
from jax.sharding import PartitionSpec as P

VGX = 16
VGY = 16
VGZ = 8
STEPS = 3
LANES = 128
LOG2E = 1.4426950408889634
MESH = pl.DeviceIdType.MESH

H1 = 3.0 / VGX
H2 = 3.0 / VGY
H3 = 3.0 / VGZ


def minmod(lower, upper):
    return jnp.maximum(jnp.minimum(lower, upper), 0.0) + jnp.minimum(
        jnp.maximum(lower, upper), 0.0
    )


def split3(value):
    high = value.astype(jnp.bfloat16).astype(jnp.float32)
    rest = value - high
    middle = rest.astype(jnp.bfloat16).astype(jnp.float32)
    return high, middle, rest - middle


def kernel(
    rows, ny, nz, width, nx_dev, nv,
    dist, order_in, codes_in, knudsen_in, inflow_in,
    out,
    state, moved, halo_low, halo_high, mom_outer, mom_inner, coef, feat, wide, cour,
    order, codes, knudsen, inflow, spread, cell_code,
    in_sem, small_sem, out_sem, halo_send, halo_recv,
    outer_send, outer_recv, inner_send, inner_recv,
):
    tiles = width // LANES
    total = float(width * nv)
    chunks = 2 * ny * nz // LANES
    yc = ny // chunks
    inner_rows = rows - 4
    inner_blocks = inner_rows * ny * nz // LANES
    yb = LANES // nz
    per_layer = ny // yb
    mx = lax.axis_index("gx")
    mv = lax.axis_index("vert")
    has_low = mx > 0
    has_high = mx < nx_dev - 1

    small = [
        pltpu.make_async_copy(source, target, small_sem.at[i])
        for i, (source, target) in enumerate(
            ((order_in, order), (codes_in, codes), (knudsen_in, knudsen), (inflow_in, inflow))
        )
    ]
    for copy in small:
        copy.start()
    load = [
        pltpu.make_async_copy(
            dist.at[pl.ds(first, count)], state.at[0, pl.ds(first, count)], in_sem.at[i]
        )
        for i, (first, count) in enumerate(((0, 2), (rows - 2, 2), (2, inner_rows)))
    ]
    for copy in load:
        copy.start()

    barrier = pltpu.get_barrier_semaphore()

    @pl.when(has_low)
    def _():
        pl.semaphore_signal(barrier, inc=1, device_id={"gx": mx - 1}, device_id_type=MESH)

    @pl.when(has_high)
    def _():
        pl.semaphore_signal(barrier, inc=1, device_id={"gx": mx + 1}, device_id_type=MESH)

    for p in range(1, nv):
        pl.semaphore_signal(
            barrier, inc=1, device_id={"vert": lax.rem(mv + p, nv)}, device_id_type=MESH
        )
    pl.semaphore_wait(
        barrier, nv - 1 + has_low.astype(jnp.int32) + has_high.astype(jnp.int32)
    )

    def to_low(t, c, source):
        ys = pl.ds(c * yc, yc)
        return pltpu.make_async_remote_copy(
            src_ref=source.at[pl.ds(0, 2), ys],
            dst_ref=halo_high.at[t, :, ys],
            send_sem=halo_send.at[t, 0, c],
            recv_sem=halo_recv.at[t, 0, c],
            device_id={"gx": mx - 1},
            device_id_type=MESH,
        )

    def to_high(t, c, source):
        ys = pl.ds(c * yc, yc)
        return pltpu.make_async_remote_copy(
            src_ref=source.at[pl.ds(rows - 2, 2), ys],
            dst_ref=halo_low.at[t, :, ys],
            send_sem=halo_send.at[t, 1, c],
            recv_sem=halo_recv.at[t, 1, c],
            device_id={"gx": mx + 1},
            device_id_type=MESH,
        )

    @pl.when(has_low)
    def _():
        for c in range(chunks):
            to_low(0, c, dist).start()

    @pl.when(has_high)
    def _():
        for c in range(chunks):
            to_high(0, c, dist).start()

    for copy in small:
        copy.wait()

    slot = order[...]
    odd1 = (2 * (slot // (VGY * VGZ)) + 1 - VGX).astype(jnp.float32)
    odd2 = (2 * ((slot // VGZ) % VGY) + 1 - VGY).astype(jnp.float32)
    odd3 = (2 * (slot % VGZ) + 1 - VGZ).astype(jnp.float32)
    ratio = (H3 / H1) ** 2
    table = jnp.concatenate(
        [
            jnp.ones_like(odd1), odd1, odd2, odd3,
            odd1 * odd1, odd2 * odd2, ratio * odd3 * odd3, jnp.zeros_like(odd1),
        ],
        axis=0,
    )
    feat[...] = jnp.concatenate([table, jnp.zeros_like(table)], axis=0).astype(jnp.bfloat16)
    keep_row = (lax.broadcasted_iota(jnp.int32, (8, LANES), 0) == 7).astype(jnp.float32)
    broad = jnp.concatenate([table, keep_row], axis=1)
    wide[...] = jnp.concatenate([broad, broad, broad, jnp.zeros_like(broad)], axis=0).astype(
        jnp.bfloat16
    )
    speeds = []
    for speed in (0.1 * H1 * odd1, (H2 / 30.0) * odd2, (H3 / 30.0) * odd3):
        gain = 0.5 * (1.0 - jnp.abs(speed)) * jnp.where(speed > 0, 1.0, -1.0)
        speeds += [speed, gain]
    cour[...] = jnp.concatenate(speeds + [jnp.zeros_like(odd1)] * 2, axis=0)

    pick = lax.broadcasted_iota(jnp.int32, (nz, LANES), 1) % nz
    pick = (pick == lax.broadcasted_iota(jnp.int32, (nz, LANES), 0)).astype(jnp.bfloat16)
    spread[...] = jnp.dot(
        codes[...].reshape(rows * ny, nz).astype(jnp.float32).astype(jnp.bfloat16),
        pick,
        preferred_element_type=jnp.float32,
    )

    def code_part(row, count, at):
        line = lax.broadcasted_iota(jnp.int32, (count, LANES), 0) + at
        lane = lax.broadcasted_iota(jnp.int32, (count, LANES), 1) // nz
        return jnp.sum(
            jnp.where(line == lane, spread[row:row + count], 0.0), axis=0, keepdims=True
        )

    for c in range(chunks):
        for side in range(2):
            row = side * (rows - 2) * ny + c * yc
            cell_code[2 * c + side] = code_part(row, yc, 0) + code_part(row + ny, yc, yc)
    for k in range(inner_blocks):
        cell_code[2 * chunks + k] = code_part(2 * ny + k * yb, yb, 0)

    @pl.when(jnp.logical_not(has_low))
    def _():
        halo_low[...] = jnp.zeros_like(halo_low)

    @pl.when(jnp.logical_not(has_high))
    def _():
        halo_high[...] = jnp.zeros_like(halo_high)

    for copy in load:
        copy.wait()

    def constants(j, dim):
        lanes = pl.ds(pl.multiple_of(j * LANES, LANES), LANES)
        speed = jnp.broadcast_to(cour[2 * dim:2 * dim + 1, lanes], (nz, LANES))
        gain = jnp.broadcast_to(cour[2 * dim + 1:2 * dim + 2, lanes], (nz, LANES))
        return lanes, speed, gain, speed > 0

    def yz_tile(now, layer, index, _):
        x = layer(index // tiles)
        lanes, speed2, gain2, ahead2 = constants(index % tiles, 1)
        _, speed3, gain3, ahead3 = constants(index % tiles, 2)

        def cell(y):
            return state[now, x, y % ny, :, lanes]

        f_low = cell(-2)
        f_mid = cell(-1)
        f = cell(0)
        d_low = f_mid - f_low
        d = f - f_mid
        l_low = f_mid + gain2 * minmod(d_low, d)
        f_up = cell(1)
        d_up = f_up - f
        l = f + gain2 * minmod(d, d_up)
        change = l - l_low
        for y in range(ny):
            f_next = cell(y + 2)
            d_next = f_next - f_up
            l_up = f_up + gain2 * minmod(d_up, d_next)
            change_up = l_up - l
            result = f - speed2 * jnp.where(ahead2, change, change_up)
            dz = pltpu.roll(f, nz - 1, 0) - f
            lz = f + gain3 * minmod(pltpu.roll(dz, 1, 0), dz)
            face = jnp.where(ahead3, lz, pltpu.roll(lz, nz - 1, 0))
            moved[x, y, :, lanes] = result - speed3 * (face - pltpu.roll(face, 1, 0))
            f, f_up = f_up, f_next
            d_up = d_next
            l, change = l_up, change_up
        return 0

    def yz(now, layer, count):
        lax.fori_loop(0, count * tiles, functools.partial(yz_tile, now, layer), 0)

    def x_tile(jobs, j, ys):
        lanes, speed, gain, ahead = constants(j, 0)
        for y in ys:
            for sources, outputs in jobs:
                f = [ref[(*lead, y, slice(None), lanes)] for ref, lead in sources]
                d = [b - a for a, b in zip(f[:-1], f[1:])]
                l = [f[i + 1] + gain * minmod(d[i], d[i + 1]) for i in range(len(d) - 1)]
                c = [b - a for a, b in zip(l[:-1], l[1:])]
                for i, x in enumerate(outputs):
                    moved[x, y, :, lanes] = moved[x, y, :, lanes] - speed * jnp.where(
                        ahead, c[i], c[i + 1]
                    )

    def x_inner(now):
        job = ([(state, (now, x)) for x in range(rows)], range(2, rows - 2))

        def tile(index, _):
            x_tile([job], index % tiles, [(index // tiles) * yc + k for k in range(yc)])
            return 0

        lax.fori_loop(0, (ny // yc) * tiles, tile, 0)

    def x_outer(t, now, chunk):
        low = [(halo_low, (t, 0)), (halo_low, (t, 1))] + [(state, (now, x)) for x in range(4)]
        high = [(state, (now, x)) for x in range(rows - 4, rows)] + [
            (halo_high, (t, 0)), (halo_high, (t, 1))
        ]
        jobs = [(low, (0, 1)), (high, (rows - 2, rows - 1))]

        def tile(j, _):
            x_tile(jobs, j, [chunk * yc + k for k in range(yc)])
            return 0

        lax.fori_loop(0, tiles, tile, 0)

    def block_moments(flat):
        high = flat.astype(jnp.bfloat16)
        low = (flat - high.astype(jnp.float32)).astype(jnp.bfloat16)
        contract = (((1,), (1,)), ((), ()))
        sums = lax.dot_general(
            feat[...], high, contract, preferred_element_type=jnp.float32
        ) + lax.dot_general(feat[...], low, contract, preferred_element_type=jnp.float32)
        return sums[0:8]

    def outer_copy(t, c, p):
        return pltpu.make_async_remote_copy(
            src_ref=mom_outer.at[t, mv, c],
            dst_ref=mom_outer.at[t, mv, c],
            send_sem=outer_send.at[t, c, p - 1],
            recv_sem=outer_recv.at[t, c, p - 1],
            device_id={"vert": lax.rem(mv + p, nv)},
            device_id_type=MESH,
        )

    def inner_copy(t, p):
        return pltpu.make_async_remote_copy(
            src_ref=mom_inner.at[t, mv],
            dst_ref=mom_inner.at[t, mv],
            send_sem=inner_send.at[t, p - 1],
            recv_sem=inner_recv.at[t, p - 1],
            device_id={"vert": lax.rem(mv + p, nv)},
            device_id_type=MESH,
        )

    def moments_outer(t, c):
        for side in range(2):
            part = moved[pl.ds(side * (rows - 2), 2), pl.ds(c * yc, yc)]
            mom_outer[t, mv, c, side] = block_moments(part.reshape(LANES, width))
        for p in range(1, nv):
            outer_copy(t, c, p).start()

    def moments_inner(t):
        def layer(i, _):
            sums = block_moments(moved[i + 2].reshape(ny * nz, width))
            for k in range(per_layer):
                mom_inner[t, mv, i * per_layer + k] = sums[:, k * LANES:(k + 1) * LANES]
            return 0

        lax.fori_loop(0, inner_rows, layer, 0)
        for p in range(1, nv):
            inner_copy(t, p).start()

    def coefficients(blocks, first):
        sums = jnp.concatenate(
            [functools.reduce(lambda a, b: a + b, parts) for parts in blocks], axis=1
        )
        count = len(blocks)
        code = jnp.concatenate([cell_code[first + k] for k in range(count)], axis=1)
        weight = sums[0:1]
        density = weight / total
        inverse = 1.0 / weight
        u1 = H1 * sums[1:2] * inverse
        u2 = H2 * sums[2:3] * inverse
        u3 = H3 * sums[3:4] * inverse
        square = (H1 * H1) * (sums[4:5] + sums[5:6] + sums[6:7]) * inverse
        temperature = (square - (u1 * u1 + u2 * u2 + u3 * u3)) / 3.0
        is_inflow = code == 1.0
        is_wall = code == 2.0
        is_open = code == 0.0
        rate = 0.5 * density / (density + knudsen[0:1, 0:1])
        zero = jnp.zeros_like(u1)
        u1 = jnp.where(is_inflow, inflow[0:1, 1:2], jnp.where(is_wall, zero, u1))
        u2 = jnp.where(is_open, u2, zero)
        u3 = jnp.where(is_open, u3, zero)
        temperature = jnp.where(
            is_inflow, inflow[0:1, 2:3], jnp.where(is_wall, inflow[0:1, 3:4], temperature)
        )
        front = jnp.where(
            is_inflow, inflow[0:1, 0:1], jnp.where(is_wall, density, rate * density)
        )
        keep = jnp.where(is_open, 1.0 - rate, zero)
        sharp = (0.5 * LOG2E) / temperature

        def axis_sum(points, spacing, u):
            grid = lax.broadcasted_iota(jnp.int32, (points, count * LANES), 0)
            away = (2.0 * grid.astype(jnp.float32) + (1.0 - points)) * spacing - u
            return jnp.sum(jnp.exp2(-(away * away) * sharp), axis=0, keepdims=True)

        norm = axis_sum(VGX, H1, u1) * axis_sum(VGY, H2, u2) * axis_sum(VGZ, H3, u3)
        constant = jnp.log2(front * total / norm) - (u1 * u1 + u2 * u2 + u3 * u3) * sharp
        slope = 2.0 * sharp
        quad = -(H1 * H1) * sharp
        packed = jnp.concatenate(
            [
                constant, slope * u1 * H1, slope * u2 * H2, slope * u3 * H3,
                quad, quad, quad, keep,
            ],
            axis=0,
        )
        stacked = jnp.concatenate([*split3(packed), jnp.zeros_like(packed)], axis=0)
        for k in range(count):
            coef[first + k] = stacked[:, k * LANES:(k + 1) * LANES].T.astype(jnp.bfloat16)

    def relax_block(then, k, xs, ys):
        power = jnp.dot(coef[k], wide[...], preferred_element_type=jnp.float32)
        keep = power[:, width:]
        for j in range(tiles):
            lanes = slice(j * LANES, (j + 1) * LANES)
            old = moved[xs, ys, :, lanes]
            new = keep * old.reshape(LANES, LANES) + jnp.exp2(power[:, lanes])
            state[then, xs, ys, :, lanes] = new.reshape(old.shape)

    def relax_outer(t, then, c):
        for p in range(1, nv):
            outer_copy(t, c, p).wait_recv()
        coefficients(
            [[mom_outer[t, v, c, side] for v in range(nv)] for side in range(2)], 2 * c
        )
        for side in range(2):
            relax_block(
                then, 2 * c + side, pl.ds(side * (rows - 2), 2), pl.ds(c * yc, yc)
            )

    def relax_inner(t, then):
        for p in range(1, nv):
            inner_copy(t, p).wait_recv()
        coefficients(
            [[mom_inner[t, v, k] for v in range(nv)] for k in range(inner_blocks)], 2 * chunks
        )

        def block(k, _):
            relax_block(
                then, 2 * chunks + k,
                pl.ds(2 + k // per_layer, 1), pl.ds((k % per_layer) * yb, yb),
            )
            return 0

        lax.fori_loop(0, inner_blocks, block, 0)

    final = STEPS % 2

    def write_inner():
        xs = pl.ds(2, inner_rows)
        return pltpu.make_async_copy(state.at[final, xs], out.at[xs], out_sem.at[0])

    def write_outer(c, side):
        xs, ys = pl.ds(side * (rows - 2), 2), pl.ds(c * yc, yc)
        return pltpu.make_async_copy(
            state.at[final, xs, ys], out.at[xs, ys], out_sem.at[1 + 2 * c + side]
        )

    def outer_layer(i):
        return i + inner_rows * (i // 2)

    def step(t, _):
        last = t == STEPS - 1
        now = t % 2
        then = 1 - now
        current = state.at[now]
        following = state.at[then]
        split = inner_rows // 2

        def fill_1():
            yz(now, lambda i: i + 2, split)

        def fill_2():
            yz(now, lambda i: i + 2 + split, inner_rows - split)

        def fill_3():
            x_inner(now)
            moments_inner(t)

        def fill_4():
            relax_inner(t, then)

        fillers = [fill_1, fill_2, fill_3, fill_4]
        yz(now, outer_layer, 4)
        for c in range(chunks):

            @pl.when(has_high)
            def _():
                to_low(t, c, current).wait_recv()

            @pl.when(has_low)
            def _():
                to_high(t, c, current).wait_recv()

            x_outer(t, now, c)
            moments_outer(t, c)
            if c < chunks - 1:
                fillers[c]()
            else:
                for fill in fillers[c:]:
                    fill()

            @pl.when(last)
            def _():
                if c == chunks - 1:
                    write_inner().start()

            relax_outer(t, then, c)

            @pl.when(jnp.logical_and(has_low, jnp.logical_not(last)))
            def _():
                to_low(t + 1, c, following).start()

            @pl.when(jnp.logical_and(has_high, jnp.logical_not(last)))
            def _():
                to_high(t + 1, c, following).start()

            @pl.when(last)
            def _():
                for side in range(2):
                    write_outer(c, side).start()

        for c in range(chunks):

            @pl.when(has_low)
            def _():
                to_low(t, c, current).wait_send()

            @pl.when(has_high)
            def _():
                to_high(t, c, current).wait_send()

            for p in range(1, nv):
                outer_copy(t, c, p).wait_send()
        for p in range(1, nv):
            inner_copy(t, p).wait_send()
        return 0

    lax.fori_loop(0, STEPS, step, 0)
    write_inner().wait()
    for c in range(chunks):
        for side in range(2):
            write_outer(c, side).wait()


def body(distribution, velocity_order, cell_codes, knudsen, inflow):
    rows, ny, nz, width = distribution.shape
    nv = lax.axis_size("vert")
    nx_dev = lax.axis_size("gx")
    chunks = 2 * ny * nz // LANES
    inner_blocks = (rows - 4) * ny * nz // LANES
    blocks = 2 * chunks + inner_blocks
    hbm = pl.BlockSpec(memory_space=pl.ANY)
    dma = pltpu.SemaphoreType.DMA
    return pl.pallas_call(
        functools.partial(kernel, rows, ny, nz, width, nx_dev, nv),
        out_shape=jax.ShapeDtypeStruct(distribution.shape, jnp.float32),
        in_specs=[pl.BlockSpec(memory_space=pltpu.HBM)] * 5,
        out_specs=hbm,
        scratch_shapes=[
            pltpu.VMEM((2, rows, ny, nz, width), jnp.float32),
            pltpu.VMEM((rows, ny, nz, width), jnp.float32),
            pltpu.VMEM((STEPS, 2, ny, nz, width), jnp.float32),
            pltpu.VMEM((STEPS, 2, ny, nz, width), jnp.float32),
            pltpu.VMEM((STEPS, nv, chunks, 2, 8, LANES), jnp.float32),
            pltpu.VMEM((STEPS, nv, inner_blocks, 8, LANES), jnp.float32),
            pltpu.VMEM((blocks, LANES, 32), jnp.bfloat16),
            pltpu.VMEM((16, width), jnp.bfloat16),
            pltpu.VMEM((32, width + LANES), jnp.bfloat16),
            pltpu.VMEM((8, width), jnp.float32),
            pltpu.VMEM((1, width), jnp.int32),
            pltpu.VMEM((rows, ny, nz), jnp.int32),
            pltpu.VMEM((1, 1), jnp.float32),
            pltpu.VMEM((1, 4), jnp.float32),
            pltpu.VMEM((rows * ny, LANES), jnp.float32),
            pltpu.VMEM((blocks, 1, LANES), jnp.float32),
            dma((3,)),
            dma((4,)),
            dma((1 + 2 * chunks,)),
            dma((STEPS, 2, chunks)),
            dma((STEPS, 2, chunks)),
            dma((STEPS, chunks, nv - 1)),
            dma((STEPS, chunks, nv - 1)),
            dma((STEPS, nv - 1)),
            dma((STEPS, nv - 1)),
        ],
        compiler_params=pltpu.CompilerParams(
            collective_id=0, has_side_effects=True, vmem_limit_bytes=48 * 1024 * 1024
        ),
    )(
        distribution,
        velocity_order.reshape(1, width),
        cell_codes,
        knudsen.reshape(1, 1),
        inflow.reshape(1, 4),
    )


def solution(mesh):
    placed = (
        P(("groups", "gx"), None, None, "vert"),
        P("vert"),
        P(("groups", "gx"), None, None),
        P("groups"),
        P("groups"),
    )
    return jax.shard_map(
        body,
        mesh=mesh,
        in_specs=placed,
        out_specs=P(("groups", "gx"), None, None, "vert"),
        check_vma=False,
    )
```

time: 77.1 us -> 77.7 us (level)
  the two profiles are of different devices: /device:TPU:1 before, /device:TPU:2 now
where the time goes in v1:
time: 77.7 us; the launch traced here: 76.7 us
  Pallas kernels  71.8 us (92%)
  local copies, waits for them, and re-layouts  4.18 us (5%)
    pallas_call x1, Pallas kernels, body(): pl.pallas_call(functools.partial(kernel, rows, ny, nz, width, nx_dev, nv)...  71.8 us
    unnamed x7, local copies, waits for them, and re-layouts  4.18 us

profile of v1, /device:TPU:2, one launch (start us, length us, event | category | flops | bytes accessed | tf_op | source)
XLA Modules:
  0.0 76.7 jit_solution(16340547949809629335)
XLA Ops:
  0.7 0.0 copy-start
  0.7 0.8 %copy-done = s32[8,16,16]{2,1,0:T(8,128)S(1)} copy-done((s32[8,16,16]{2,1,0:T(8,128)S(1)}, s32[8,16,16]{2,1,0:T(8,128)}, u32[]{:S(2)}) %copy-start) | copy-done | bytes 8216
  1.5 0.0 copy-start.1
  1.5 0.7 copy-done.1
  2.2 0.0 copy-start.2
  2.2 0.7 copy-done.2
  2.8 71.8 %shard_map.55 = f32[8,16,16,512]{3,2,1,0:T(8,128)S(1)} custom-call(f32[8,16,16,512]{3,2,1,0:T(8,128)} %dist.1, s32[1,512]{1,0:T(1,128)S(1)} %bitcast.4, s32[8,16,16]{2,1,0:T(8,128)S(1)} %copy-done, f32[1,1]{1,0:T(1,128)} %bitcast.3.knudsen_in, f32[1,4]{1,0:T(1,128)S(1)} %bitcast.5), custom_call_target="tpu_custom_call" | custom-call | tf_op jit(solution)/shard_map/pallas_call | solution.py:504
  74.6 2.0 %copy.8 = f32[8,16,16,512]{3,2,1,0:T(8,128)} copy(f32[8,16,16,512]{3,2,1,0:T(8,128)S(1)} %shard_map.55) | data formatting | bytes 8388608
Async XLA Ops:
  0.7 0.8 %copy-start = (s32[8,16,16]{2,1,0:T(8,128)S(1)}, s32[8,16,16]{2,1,0:T(8,128)}, u32[]{:S(2)}) copy-start(s32[8,16,16]{2,1,0:T(8,128)} %codes_in.1) | copy-start | bytes 24580
  1.5 0.7 copy-start.1
  2.2 0.7 copy-start.2

commit v2 on v1

--- a/solution.py
+++ b/solution.py
@@ -21,9 +21,7 @@
 
 
 def minmod(lower, upper):
-    return jnp.maximum(jnp.minimum(lower, upper), 0.0) + jnp.minimum(
-        jnp.maximum(lower, upper), 0.0
-    )
+    return jnp.maximum(jnp.minimum(lower, upper), jnp.minimum(jnp.maximum(lower, upper), 0.0))
 
 
 def split3(value):
@@ -37,19 +35,18 @@
     rows, ny, nz, width, nx_dev, nv,
     dist, order_in, codes_in, knudsen_in, inflow_in,
     out,
-    state, moved, halo_low, halo_high, mom_outer, mom_inner, coef, feat, wide, cour,
+    state, part, moved, halo_low, halo_high, mom_outer, mom_inner, coef, feat, wide, cour,
     order, codes, knudsen, inflow, spread, cell_code,
     in_sem, small_sem, out_sem, halo_send, halo_recv,
     outer_send, outer_recv, inner_send, inner_recv,
 ):
     tiles = width // LANES
     total = float(width * nv)
-    chunks = 2 * ny * nz // LANES
-    yc = ny // chunks
+    yc = LANES // nz
+    chunks = ny // yc
     inner_rows = rows - 4
-    inner_blocks = inner_rows * ny * nz // LANES
-    yb = LANES // nz
-    per_layer = ny // yb
+    inner_blocks = inner_rows * chunks
+    outer_layers = (0, 1, rows - 2, rows - 1)
     mx = lax.axis_index("gx")
     mv = lax.axis_index("vert")
     has_low = mx > 0
@@ -137,7 +134,8 @@
         ],
         axis=0,
     )
-    feat[...] = jnp.concatenate([table, jnp.zeros_like(table)], axis=0).astype(jnp.bfloat16)
+    rest = jnp.zeros((LANES - 8, width), jnp.float32)
+    feat[...] = jnp.concatenate([table, rest], axis=0).T.astype(jnp.bfloat16)
     keep_row = (lax.broadcasted_iota(jnp.int32, (8, LANES), 0) == 7).astype(jnp.float32)
     broad = jnp.concatenate([table, keep_row], axis=1)
     wide[...] = jnp.concatenate([broad, broad, broad, jnp.zeros_like(broad)], axis=0).astype(
@@ -157,19 +155,15 @@
         preferred_element_type=jnp.float32,
     )
 
-    def code_part(row, count, at):
-        line = lax.broadcasted_iota(jnp.int32, (count, LANES), 0) + at
-        lane = lax.broadcasted_iota(jnp.int32, (count, LANES), 1) // nz
-        return jnp.sum(
-            jnp.where(line == lane, spread[row:row + count], 0.0), axis=0, keepdims=True
-        )
-
-    for c in range(chunks):
-        for side in range(2):
-            row = side * (rows - 2) * ny + c * yc
-            cell_code[2 * c + side] = code_part(row, yc, 0) + code_part(row + ny, yc, yc)
-    for k in range(inner_blocks):
-        cell_code[2 * chunks + k] = code_part(2 * ny + k * yb, yb, 0)
+    own_line = lax.broadcasted_iota(jnp.int32, (yc, LANES), 0)
+    own_line = own_line == lax.broadcasted_iota(jnp.int32, (yc, LANES), 1) // nz
+    places = [(x, c) for c in range(chunks) for x in outer_layers]
+    places += [(x, c) for x in range(2, rows - 2) for c in range(chunks)]
+    for k, (x, c) in enumerate(places):
+        row = x * ny + c * yc
+        cell_code[k] = jnp.sum(
+            jnp.where(own_line, spread[row:row + yc], 0.0), axis=0, keepdims=True
+        )
 
     @pl.when(jnp.logical_not(has_low))
     def _():
@@ -193,21 +187,15 @@
         lanes, speed2, gain2, ahead2 = constants(index % tiles, 1)
         _, speed3, gain3, ahead3 = constants(index % tiles, 2)
 
-        def cell(y):
-            return state[now, x, y % ny, :, lanes]
-
-        f_low = cell(-2)
-        f_mid = cell(-1)
-        f = cell(0)
-        d_low = f_mid - f_low
+        cells = [state[now, x, y, :, lanes] for y in range(ny)]
+        f_low, f_mid, f, f_up = cells[-2], cells[-1], cells[0], cells[1]
         d = f - f_mid
-        l_low = f_mid + gain2 * minmod(d_low, d)
-        f_up = cell(1)
+        l_low = f_mid + gain2 * minmod(f_mid - f_low, d)
         d_up = f_up - f
         l = f + gain2 * minmod(d, d_up)
         change = l - l_low
         for y in range(ny):
-            f_next = cell(y + 2)
+            f, f_up, f_next = cells[y], cells[(y + 1) % ny], cells[(y + 2) % ny]
             d_next = f_next - f_up
             l_up = f_up + gain2 * minmod(d_up, d_next)
             change_up = l_up - l
@@ -215,8 +203,7 @@
             dz = pltpu.roll(f, nz - 1, 0) - f
             lz = f + gain3 * minmod(pltpu.roll(dz, 1, 0), dz)
             face = jnp.where(ahead3, lz, pltpu.roll(lz, nz - 1, 0))
-            moved[x, y, :, lanes] = result - speed3 * (face - pltpu.roll(face, 1, 0))
-            f, f_up = f_up, f_next
+            part[x, y, :, lanes] = result - speed3 * (face - pltpu.roll(face, 1, 0))
             d_up = d_next
             l, change = l_up, change_up
         return 0
@@ -233,18 +220,20 @@
                 l = [f[i + 1] + gain * minmod(d[i], d[i + 1]) for i in range(len(d) - 1)]
                 c = [b - a for a, b in zip(l[:-1], l[1:])]
                 for i, x in enumerate(outputs):
-                    moved[x, y, :, lanes] = moved[x, y, :, lanes] - speed * jnp.where(
+                    moved[x, y, :, lanes] = part[x, y, :, lanes] - speed * jnp.where(
                         ahead, c[i], c[i + 1]
                     )
 
+    yu = yc // 2
+
     def x_inner(now):
         job = ([(state, (now, x)) for x in range(rows)], range(2, rows - 2))
 
         def tile(index, _):
-            x_tile([job], index % tiles, [(index // tiles) * yc + k for k in range(yc)])
+            x_tile([job], index % tiles, [(index // tiles) * yu + k for k in range(yu)])
             return 0
 
-        lax.fori_loop(0, (ny // yc) * tiles, tile, 0)
+        lax.fori_loop(0, (ny // yu) * tiles, tile, 0)
 
     def x_outer(t, now, chunk):
         low = [(halo_low, (t, 0)), (halo_low, (t, 1))] + [(state, (now, x)) for x in range(4)]
@@ -253,20 +242,21 @@
         ]
         jobs = [(low, (0, 1)), (high, (rows - 2, rows - 1))]
 
-        def tile(j, _):
-            x_tile(jobs, j, [chunk * yc + k for k in range(yc)])
+        def tile(index, _):
+            first = chunk * yc + (index // tiles) * yu
+            x_tile(jobs, index % tiles, [first + k for k in range(yu)])
             return 0
 
-        lax.fori_loop(0, tiles, tile, 0)
-
-    def block_moments(flat):
+        lax.fori_loop(0, (yc // yu) * tiles, tile, 0)
+
+    def block_moments(x, c):
+        flat = moved[x, pl.ds(c * yc, yc)].reshape(LANES, width)
         high = flat.astype(jnp.bfloat16)
         low = (flat - high.astype(jnp.float32)).astype(jnp.bfloat16)
-        contract = (((1,), (1,)), ((), ()))
-        sums = lax.dot_general(
-            feat[...], high, contract, preferred_element_type=jnp.float32
-        ) + lax.dot_general(feat[...], low, contract, preferred_element_type=jnp.float32)
-        return sums[0:8]
+        sums = jnp.dot(high, feat[...], preferred_element_type=jnp.float32) + jnp.dot(
+            low, feat[...], preferred_element_type=jnp.float32
+        )
+        return sums.T[0:8]
 
     def outer_copy(t, c, p):
         return pltpu.make_async_remote_copy(
@@ -289,17 +279,15 @@
         )
 
     def moments_outer(t, c):
-        for side in range(2):
-            part = moved[pl.ds(side * (rows - 2), 2), pl.ds(c * yc, yc)]
-            mom_outer[t, mv, c, side] = block_moments(part.reshape(LANES, width))
+        for i, x in enumerate(outer_layers):
+            mom_outer[t, mv, c, i] = block_moments(x, c)
         for p in range(1, nv):
             outer_copy(t, c, p).start()
 
     def moments_inner(t):
         def layer(i, _):
-            sums = block_moments(moved[i + 2].reshape(ny * nz, width))
-            for k in range(per_layer):
-                mom_inner[t, mv, i * per_layer + k] = sums[:, k * LANES:(k + 1) * LANES]
+            for c in range(chunks):
+                mom_inner[t, mv, i * chunks + c] = block_moments(i + 2, c)
             return 0
 
         lax.fori_loop(0, inner_rows, layer, 0)
@@ -357,41 +345,38 @@
         for k in range(count):
             coef[first + k] = stacked[:, k * LANES:(k + 1) * LANES].T.astype(jnp.bfloat16)
 
-    def relax_block(then, k, xs, ys):
+    def relax_block(then, k, x, c):
+        ys = pl.ds(c * yc, yc)
         power = jnp.dot(coef[k], wide[...], preferred_element_type=jnp.float32)
         keep = power[:, width:]
         for j in range(tiles):
             lanes = slice(j * LANES, (j + 1) * LANES)
-            old = moved[xs, ys, :, lanes]
+            old = moved[x, ys, :, lanes]
             new = keep * old.reshape(LANES, LANES) + jnp.exp2(power[:, lanes])
-            state[then, xs, ys, :, lanes] = new.reshape(old.shape)
+            state[then, x, ys, :, lanes] = new.reshape(old.shape)
 
     def relax_outer(t, then, c):
         for p in range(1, nv):
             outer_copy(t, c, p).wait_recv()
         coefficients(
-            [[mom_outer[t, v, c, side] for v in range(nv)] for side in range(2)], 2 * c
-        )
-        for side in range(2):
-            relax_block(
-                then, 2 * c + side, pl.ds(side * (rows - 2), 2), pl.ds(c * yc, yc)
-            )
+            [[mom_outer[t, v, c, i] for v in range(nv)] for i in range(4)], 4 * c
+        )
+        for i, x in enumerate(outer_layers):
+            relax_block(then, 4 * c + i, x, c)
 
     def relax_inner(t, then):
         for p in range(1, nv):
             inner_copy(t, p).wait_recv()
         coefficients(
-            [[mom_inner[t, v, k] for v in range(nv)] for k in range(inner_blocks)], 2 * chunks
-        )
-
-        def block(k, _):
-            relax_block(
-                then, 2 * chunks + k,
-                pl.ds(2 + k // per_layer, 1), pl.ds((k % per_layer) * yb, yb),
-            )
+            [[mom_inner[t, v, k] for v in range(nv)] for k in range(inner_blocks)], 4 * chunks
+        )
+
+        def layer(i, _):
+            for c in range(chunks):
+                relax_block(then, 4 * chunks + i * chunks + c, i + 2, c)
             return 0
 
-        lax.fori_loop(0, inner_blocks, block, 0)
+        lax.fori_loop(0, inner_rows, layer, 0)
 
     final = STEPS % 2
 
@@ -416,20 +401,17 @@
         following = state.at[then]
         split = inner_rows // 2
 
-        def fill_1():
+        def fill_early():
             yz(now, lambda i: i + 2, split)
 
-        def fill_2():
+        def fill_between():
             yz(now, lambda i: i + 2 + split, inner_rows - split)
-
-        def fill_3():
             x_inner(now)
             moments_inner(t)
 
-        def fill_4():
+        def fill_late():
             relax_inner(t, then)
 
-        fillers = [fill_1, fill_2, fill_3, fill_4]
         yz(now, outer_layer, 4)
         for c in range(chunks):
 
@@ -443,11 +425,10 @@
 
             x_outer(t, now, c)
             moments_outer(t, c)
-            if c < chunks - 1:
-                fillers[c]()
-            else:
-                for fill in fillers[c:]:
-                    fill()
+            if c == 0:
+                fill_early()
+            if c == chunks - 1:
+                fill_late()
 
             @pl.when(last)
             def _():
@@ -468,6 +449,9 @@
             def _():
                 for side in range(2):
                     write_outer(c, side).start()
+
+            if c == 0:
+                fill_between()
 
         for c in range(chunks):
 
@@ -496,9 +480,9 @@
     rows, ny, nz, width = distribution.shape
     nv = lax.axis_size("vert")
     nx_dev = lax.axis_size("gx")
-    chunks = 2 * ny * nz // LANES
-    inner_blocks = (rows - 4) * ny * nz // LANES
-    blocks = 2 * chunks + inner_blocks
+    chunks = ny * nz // LANES
+    inner_blocks = (rows - 4) * chunks
+    blocks = 4 * chunks + inner_blocks
     hbm = pl.BlockSpec(memory_space=pl.ANY)
     dma = pltpu.SemaphoreType.DMA
     return pl.pallas_call(
@@ -509,12 +493,13 @@
         scratch_shapes=[
             pltpu.VMEM((2, rows, ny, nz, width), jnp.float32),
             pltpu.VMEM((rows, ny, nz, width), jnp.float32),
+            pltpu.VMEM((rows, ny, nz, width), jnp.float32),
             pltpu.VMEM((STEPS, 2, ny, nz, width), jnp.float32),
             pltpu.VMEM((STEPS, 2, ny, nz, width), jnp.float32),
-            pltpu.VMEM((STEPS, nv, chunks, 2, 8, LANES), jnp.float32),
+            pltpu.VMEM((STEPS, nv, chunks, 4, 8, LANES), jnp.float32),
             pltpu.VMEM((STEPS, nv, inner_blocks, 8, LANES), jnp.float32),
             pltpu.VMEM((blocks, LANES, 32), jnp.bfloat16),
-            pltpu.VMEM((16, width), jnp.bfloat16),
+            pltpu.VMEM((width, LANES), jnp.bfloat16),
             pltpu.VMEM((32, width + LANES), jnp.bfloat16),
             pltpu.VMEM((8, width), jnp.float32),
             pltpu.VMEM((1, width), jnp.int32),

time: 77.7 us -> 68.3 us (0.88); the launches traced: 76.7 us -> 68.2 us
  Pallas kernels: 71.8 us -> 63.3 us
    pallas_call x1, Pallas kernels: 71.8 us -> 63.3 us  [body(): pl.pallas_call(functools.partial(kernel, rows, ny, nz, width, nx_dev, nv)...]
where the time goes in v2:
time: 68.3 us; the launch traced here: 68.2 us
  Pallas kernels  63.3 us (93%)
  local copies, waits for them, and re-layouts  4.18 us (6%)
    pallas_call x1, Pallas kernels, body(): pl.pallas_call(functools.partial(kernel, rows, ny, nz, width, nx_dev, nv)...  63.3 us
    unnamed x7, local copies, waits for them, and re-layouts  4.18 us

profile of v2, /device:TPU:2, one launch (start us, length us, event | category | flops | bytes accessed | tf_op | source)
XLA Modules:
  0.0 68.2 jit_solution(486691772788146183)
XLA Ops:
  0.7 0.0 copy-start
  0.7 0.8 %copy-done = s32[8,16,16]{2,1,0:T(8,128)S(1)} copy-done((s32[8,16,16]{2,1,0:T(8,128)S(1)}, s32[8,16,16]{2,1,0:T(8,128)}, u32[]{:S(2)}) %copy-start) | copy-done | bytes 8216
  1.5 0.0 copy-start.1
  1.5 0.7 copy-done.1
  2.2 0.0 copy-start.2
  2.2 0.7 copy-done.2
  2.8 63.3 %shard_map.55 = f32[8,16,16,512]{3,2,1,0:T(8,128)S(1)} custom-call(f32[8,16,16,512]{3,2,1,0:T(8,128)} %dist.1, s32[1,512]{1,0:T(1,128)S(1)} %bitcast.4, s32[8,16,16]{2,1,0:T(8,128)S(1)} %copy-done, f32[1,1]{1,0:T(1,128)} %bitcast.3.knudsen_in, f32[1,4]{1,0:T(1,128)S(1)} %bitcast.5), custom_call_target="tpu_custom_call" | custom-call | tf_op jit(solution)/shard_map/pallas_call | solution.py:488
  66.1 2.0 %copy.8 = f32[8,16,16,512]{3,2,1,0:T(8,128)} copy(f32[8,16,16,512]{3,2,1,0:T(8,128)S(1)} %shard_map.55) | data formatting | bytes 8388608
Async XLA Ops:
  0.7 0.8 %copy-start = (s32[8,16,16]{2,1,0:T(8,128)S(1)}, s32[8,16,16]{2,1,0:T(8,128)}, u32[]{:S(2)}) copy-start(s32[8,16,16]{2,1,0:T(8,128)} %codes_in.1) | copy-start | bytes 24580
  1.5 0.7 %copy-start.1 = (s32[512]{0:T(512)S(1)}, s32[512]{0:T(512)}, u32[]{:S(2)}) copy-start(s32[512]{0:T(512)} %param.6) | copy-start | bytes 6148
  2.2 0.7 copy-start.2

commit v3 on v2

--- a/solution.py
+++ b/solution.py
@@ -89,35 +89,59 @@
 
     def to_low(t, c, source):
         ys = pl.ds(c * yc, yc)
-        return pltpu.make_async_remote_copy(
-            src_ref=source.at[pl.ds(0, 2), ys],
-            dst_ref=halo_high.at[t, :, ys],
-            send_sem=halo_send.at[t, 0, c],
-            recv_sem=halo_recv.at[t, 0, c],
-            device_id={"gx": mx - 1},
-            device_id_type=MESH,
-        )
+        return [
+            pltpu.make_async_remote_copy(
+                src_ref=source.at[i, ys],
+                dst_ref=halo_high.at[t, i, ys],
+                send_sem=halo_send.at[t, 0, c, i],
+                recv_sem=halo_recv.at[t, 0, c, i],
+                device_id={"gx": mx - 1},
+                device_id_type=MESH,
+            )
+            for i in range(2)
+        ]
 
     def to_high(t, c, source):
         ys = pl.ds(c * yc, yc)
-        return pltpu.make_async_remote_copy(
-            src_ref=source.at[pl.ds(rows - 2, 2), ys],
-            dst_ref=halo_low.at[t, :, ys],
-            send_sem=halo_send.at[t, 1, c],
-            recv_sem=halo_recv.at[t, 1, c],
-            device_id={"gx": mx + 1},
-            device_id_type=MESH,
-        )
-
-    @pl.when(has_low)
-    def _():
-        for c in range(chunks):
-            to_low(0, c, dist).start()
-
-    @pl.when(has_high)
-    def _():
-        for c in range(chunks):
-            to_high(0, c, dist).start()
+        return [
+            pltpu.make_async_remote_copy(
+                src_ref=source.at[rows - 2 + i, ys],
+                dst_ref=halo_low.at[t, i, ys],
+                send_sem=halo_send.at[t, 1, c, i],
+                recv_sem=halo_recv.at[t, 1, c, i],
+                device_id={"gx": mx + 1},
+                device_id_type=MESH,
+            )
+            for i in range(2)
+        ]
+
+    crosses_high = mx % 2 == 1
+
+    def send_halo(t, parts, source, allowed):
+        def start_high():
+            for c in parts:
+                for copy in to_high(t, c, source):
+                    copy.start()
+
+        @pl.when(jnp.logical_and(allowed, jnp.logical_and(has_high, crosses_high)))
+        def _():
+            start_high()
+
+        @pl.when(jnp.logical_and(allowed, has_low))
+        def _():
+            for c in parts:
+                for copy in to_low(t, c, source):
+                    copy.start()
+
+        @pl.when(
+            jnp.logical_and(
+                allowed, jnp.logical_and(has_high, jnp.logical_not(crosses_high))
+            )
+        )
+        def _():
+            start_high()
+
+    send_halo(0, range(chunks), dist, mx >= 0)
 
     for copy in small:
         copy.wait()
@@ -417,11 +441,13 @@
 
             @pl.when(has_high)
             def _():
-                to_low(t, c, current).wait_recv()
+                for copy in to_low(t, c, current):
+                    copy.wait_recv()
 
             @pl.when(has_low)
             def _():
-                to_high(t, c, current).wait_recv()
+                for copy in to_high(t, c, current):
+                    copy.wait_recv()
 
             x_outer(t, now, c)
             moments_outer(t, c)
@@ -437,13 +463,7 @@
 
             relax_outer(t, then, c)
 
-            @pl.when(jnp.logical_and(has_low, jnp.logical_not(last)))
-            def _():
-                to_low(t + 1, c, following).start()
-
-            @pl.when(jnp.logical_and(has_high, jnp.logical_not(last)))
-            def _():
-                to_high(t + 1, c, following).start()
+            send_halo(t + 1, [c], following, jnp.logical_not(last))
 
             @pl.when(last)
             def _():
@@ -457,11 +477,13 @@
 
             @pl.when(has_low)
             def _():
-                to_low(t, c, current).wait_send()
+                for copy in to_low(t, c, current):
+                    copy.wait_send()
 
             @pl.when(has_high)
             def _():
-                to_high(t, c, current).wait_send()
+                for copy in to_high(t, c, current):
+                    copy.wait_send()
 
             for p in range(1, nv):
                 outer_copy(t, c, p).wait_send()
@@ -511,15 +533,15 @@
             dma((3,)),
             dma((4,)),
             dma((1 + 2 * chunks,)),
-            dma((STEPS, 2, chunks)),
-            dma((STEPS, 2, chunks)),
+            dma((STEPS, 2, chunks, 2)),
+            dma((STEPS, 2, chunks, 2)),
             dma((STEPS, chunks, nv - 1)),
             dma((STEPS, chunks, nv - 1)),
             dma((STEPS, nv - 1)),
             dma((STEPS, nv - 1)),
         ],
         compiler_params=pltpu.CompilerParams(
-            collective_id=0, has_side_effects=True, vmem_limit_bytes=48 * 1024 * 1024
+            collective_id=0, has_side_effects=True, vmem_limit_bytes=62 * 1024 * 1024
         ),
     )(
         distribution,

time: 68.3 us -> 70.1 us (1.026)
  Pallas kernels: 63.3 us -> 64.2 us
  local copies, waits for them, and re-layouts: 4.18 us -> 5.04 us
    pallas_call x1, Pallas kernels: 63.3 us -> 64.2 us  [body(): pl.pallas_call(functools.partial(kernel, rows, ny, nz, width, nx_dev, nv)...]
    unnamed x7 -> x1, local copies, waits for them, and re-layouts: 4.18 us -> 5.04 us
where the time goes in v3:
time: 70.1 us; the launch traced here: 69.9 us
  Pallas kernels  64.2 us (92%)
  local copies, waits for them, and re-layouts  5.04 us (7%)
    pallas_call x1, Pallas kernels, body(): pl.pallas_call(functools.partial(kernel, rows, ny, nz, width, nx_dev, nv)...  64.2 us
    unnamed x1, local copies, waits for them, and re-layouts  5.04 us

profile of v3, /device:TPU:2, one launch (start us, length us, event | category | flops | bytes accessed | tf_op | source)
XLA Modules:
  0.0 69.9 jit_solution(582254140773951053)
XLA Ops:
  0.7 64.2 %shard_map.55 = f32[8,16,16,512]{3,2,1,0:T(8,128)} custom-call(f32[8,16,16,512]{3,2,1,0:T(8,128)} %dist.1, s32[1,512]{1,0:T(1,128)} %bitcast.4, s32[8,16,16]{2,1,0:T(8,128)} %codes_in.1, f32[1,1]{1,0:T(1,128)} %bitcast.3.knudsen_in, f32[1,4]{1,0:T(1,128)} %bitcast.5), custom_call_target="tpu_custom_call" | custom-call | tf_op jit(solution)/shard_map/pallas_call | solution.py:510
  64.9 5.0 %copy.8 = f32[8,16,16,512]{3,2,1,0:T(8,128)} copy(f32[8,16,16,512]{3,2,1,0:T(8,128)} %shard_map.55) | data formatting | bytes 8388608

commit v4 on v3

--- a/solution.py
+++ b/solution.py
@@ -33,10 +33,10 @@
 
 def kernel(
     rows, ny, nz, width, nx_dev, nv,
-    dist, order_in, codes_in, knudsen_in, inflow_in,
+    dist, scalars_in, codes_in,
     out,
     state, part, moved, halo_low, halo_high, mom_outer, mom_inner, coef, feat, wide, cour,
-    order, codes, knudsen, inflow, spread, cell_code,
+    scalars, codes, spread, cell_code,
     in_sem, small_sem, out_sem, halo_send, halo_recv,
     outer_send, outer_recv, inner_send, inner_recv,
 ):
@@ -55,7 +55,7 @@
     small = [
         pltpu.make_async_copy(source, target, small_sem.at[i])
         for i, (source, target) in enumerate(
-            ((order_in, order), (codes_in, codes), (knudsen_in, knudsen), (inflow_in, inflow))
+            ((scalars_in, scalars), (codes_in, codes))
         )
     ]
     for copy in small:
@@ -146,7 +146,9 @@
     for copy in small:
         copy.wait()
 
-    slot = order[...]
+    slot = scalars[:, :width].astype(jnp.int32)
+    inflow = scalars[:, width:width + 4]
+    knudsen = scalars[:, width + 4:width + 5]
     odd1 = (2 * (slot // (VGY * VGZ)) + 1 - VGX).astype(jnp.float32)
     odd2 = (2 * ((slot // VGZ) % VGY) + 1 - VGY).astype(jnp.float32)
     odd3 = (2 * (slot % VGZ) + 1 - VGZ).astype(jnp.float32)
@@ -273,14 +275,18 @@
 
         lax.fori_loop(0, (yc // yu) * tiles, tile, 0)
 
-    def block_moments(x, c):
-        flat = moved[x, pl.ds(c * yc, yc)].reshape(LANES, width)
+    def block_moments(places):
+        flat = jnp.concatenate(
+            [moved[x, pl.ds(c * yc, yc)].reshape(LANES, width) for x, c in places], axis=0
+        )
         high = flat.astype(jnp.bfloat16)
         low = (flat - high.astype(jnp.float32)).astype(jnp.bfloat16)
-        sums = jnp.dot(high, feat[...], preferred_element_type=jnp.float32) + jnp.dot(
-            low, feat[...], preferred_element_type=jnp.float32
-        )
-        return sums.T[0:8]
+        sums = jnp.dot(
+            jnp.concatenate([high, low], axis=0), feat[...], preferred_element_type=jnp.float32
+        )
+        count = len(places) * LANES
+        sums = sums[:count] + sums[count:]
+        return [sums[k * LANES:(k + 1) * LANES].T[0:8] for k in range(len(places))]
 
     def outer_copy(t, c, p):
         return pltpu.make_async_remote_copy(
@@ -303,15 +309,15 @@
         )
 
     def moments_outer(t, c):
-        for i, x in enumerate(outer_layers):
-            mom_outer[t, mv, c, i] = block_moments(x, c)
+        for i, sums in enumerate(block_moments([(x, c) for x in outer_layers])):
+            mom_outer[t, mv, c, i] = sums
         for p in range(1, nv):
             outer_copy(t, c, p).start()
 
     def moments_inner(t):
         def layer(i, _):
-            for c in range(chunks):
-                mom_inner[t, mv, i * chunks + c] = block_moments(i + 2, c)
+            for c, sums in enumerate(block_moments([(i + 2, c) for c in range(chunks)])):
+                mom_inner[t, mv, i * chunks + c] = sums
             return 0
 
         lax.fori_loop(0, inner_rows, layer, 0)
@@ -335,7 +341,7 @@
         is_inflow = code == 1.0
         is_wall = code == 2.0
         is_open = code == 0.0
-        rate = 0.5 * density / (density + knudsen[0:1, 0:1])
+        rate = 0.5 * density / (density + knudsen)
         zero = jnp.zeros_like(u1)
         u1 = jnp.where(is_inflow, inflow[0:1, 1:2], jnp.where(is_wall, zero, u1))
         u2 = jnp.where(is_open, u2, zero)
@@ -369,15 +375,22 @@
         for k in range(count):
             coef[first + k] = stacked[:, k * LANES:(k + 1) * LANES].T.astype(jnp.bfloat16)
 
-    def relax_block(then, k, x, c):
-        ys = pl.ds(c * yc, yc)
-        power = jnp.dot(coef[k], wide[...], preferred_element_type=jnp.float32)
-        keep = power[:, width:]
-        for j in range(tiles):
-            lanes = slice(j * LANES, (j + 1) * LANES)
-            old = moved[x, ys, :, lanes]
-            new = keep * old.reshape(LANES, LANES) + jnp.exp2(power[:, lanes])
-            state[then, x, ys, :, lanes] = new.reshape(old.shape)
+    def relax_blocks(then, first, places):
+        count = len(places)
+        power = jnp.dot(
+            coef[pl.ds(first, count)].reshape(count * LANES, 32),
+            wide[...],
+            preferred_element_type=jnp.float32,
+        )
+        for k, (x, c) in enumerate(places):
+            cells = slice(k * LANES, (k + 1) * LANES)
+            ys = pl.ds(c * yc, yc)
+            keep = power[cells, width:]
+            for j in range(tiles):
+                lanes = slice(j * LANES, (j + 1) * LANES)
+                old = moved[x, ys, :, lanes]
+                new = keep * old.reshape(LANES, LANES) + jnp.exp2(power[cells, lanes])
+                state[then, x, ys, :, lanes] = new.reshape(old.shape)
 
     def relax_outer(t, then, c):
         for p in range(1, nv):
@@ -385,22 +398,23 @@
         coefficients(
             [[mom_outer[t, v, c, i] for v in range(nv)] for i in range(4)], 4 * c
         )
-        for i, x in enumerate(outer_layers):
-            relax_block(then, 4 * c + i, x, c)
-
-    def relax_inner(t, then):
+        relax_blocks(then, 4 * c, [(x, c) for x in outer_layers])
+
+    def prepare_inner(t):
         for p in range(1, nv):
             inner_copy(t, p).wait_recv()
         coefficients(
             [[mom_inner[t, v, k] for v in range(nv)] for k in range(inner_blocks)], 4 * chunks
         )
 
+    def relax_inner(then, first, count):
         def layer(i, _):
-            for c in range(chunks):
-                relax_block(then, 4 * chunks + i * chunks + c, i + 2, c)
+            relax_blocks(
+                then, 4 * chunks + i * chunks, [(i + 2, c) for c in range(chunks)]
+            )
             return 0
 
-        lax.fori_loop(0, inner_rows, layer, 0)
+        lax.fori_loop(first, first + count, layer, 0)
 
     final = STEPS % 2
 
@@ -434,7 +448,8 @@
             moments_inner(t)
 
         def fill_late():
-            relax_inner(t, then)
+            prepare_inner(t)
+            relax_inner(then, 0, split)
 
         yz(now, outer_layer, 4)
         for c in range(chunks):
@@ -456,11 +471,6 @@
             if c == chunks - 1:
                 fill_late()
 
-            @pl.when(last)
-            def _():
-                if c == chunks - 1:
-                    write_inner().start()
-
             relax_outer(t, then, c)
 
             send_halo(t + 1, [c], following, jnp.logical_not(last))
@@ -472,6 +482,12 @@
 
             if c == 0:
                 fill_between()
+            if c == chunks - 1:
+                relax_inner(then, split, inner_rows - split)
+
+                @pl.when(last)
+                def _():
+                    write_inner().start()
 
         for c in range(chunks):
 
@@ -505,12 +521,20 @@
     chunks = ny * nz // LANES
     inner_blocks = (rows - 4) * chunks
     blocks = 4 * chunks + inner_blocks
+    scalars = jnp.concatenate(
+        [
+            velocity_order.astype(jnp.float32),
+            inflow,
+            knudsen,
+            jnp.zeros((LANES - 5,), jnp.float32),
+        ]
+    )
     hbm = pl.BlockSpec(memory_space=pl.ANY)
     dma = pltpu.SemaphoreType.DMA
     return pl.pallas_call(
         functools.partial(kernel, rows, ny, nz, width, nx_dev, nv),
         out_shape=jax.ShapeDtypeStruct(distribution.shape, jnp.float32),
-        in_specs=[pl.BlockSpec(memory_space=pltpu.HBM)] * 5,
+        in_specs=[hbm] * 3,
         out_specs=hbm,
         scratch_shapes=[
             pltpu.VMEM((2, rows, ny, nz, width), jnp.float32),
@@ -524,14 +548,12 @@
             pltpu.VMEM((width, LANES), jnp.bfloat16),
             pltpu.VMEM((32, width + LANES), jnp.bfloat16),
             pltpu.VMEM((8, width), jnp.float32),
-            pltpu.VMEM((1, width), jnp.int32),
+            pltpu.VMEM((1, width + LANES), jnp.float32),
             pltpu.VMEM((rows, ny, nz), jnp.int32),
-            pltpu.VMEM((1, 1), jnp.float32),
-            pltpu.VMEM((1, 4), jnp.float32),
             pltpu.VMEM((rows * ny, LANES), jnp.float32),
             pltpu.VMEM((blocks, 1, LANES), jnp.float32),
             dma((3,)),
-            dma((4,)),
+            dma((2,)),
             dma((1 + 2 * chunks,)),
             dma((STEPS, 2, chunks, 2)),
             dma((STEPS, 2, chunks, 2)),
@@ -541,14 +563,12 @@
             dma((STEPS, nv - 1)),
         ],
         compiler_params=pltpu.CompilerParams(
-            collective_id=0, has_side_effects=True, vmem_limit_bytes=62 * 1024 * 1024
+            collective_id=0, has_side_effects=True, vmem_limit_bytes=48 * 1024 * 1024
         ),
     )(
         distribution,
-        velocity_order.reshape(1, width),
+        scalars.reshape(1, -1),
         cell_codes,
-        knudsen.reshape(1, 1),
-        inflow.reshape(1, 4),
     )
 
 

time: 70.1 us -> 70.7 us (level)
  local copies, waits for them, and re-layouts: 5.04 us -> 2.86 us
  other arithmetic: 0 us -> 1.42 us
  Pallas kernels: 64.2 us -> 65.6 us
    unnamed x1 -> x3, local copies, waits for them, and re-layouts: 5.04 us -> 2.86 us
    pallas_call x1, Pallas kernels: 64.2 us -> 65.6 us  [body(): pl.pallas_call(functools.partial(kernel, rows, ny, nz, width, nx_dev, nv)...]
    concatenate x0 -> x1, other arithmetic: none -> 0.73 us  [body(): jnp.concatenate([velocity_order.astype(jnp.float32), inflow, knudsen, jnp...]
where the time goes in v4:
time: 70.7 us; the launch traced here: 70.5 us
  Pallas kernels  65.6 us (93%)
  local copies, waits for them, and re-layouts  2.86 us (4%)
  other arithmetic  1.42 us (2%)
    pallas_call x1, Pallas kernels, body(): pl.pallas_call(functools.partial(kernel, rows, ny, nz, width, nx_dev, nv)...  65.6 us
    unnamed x3, local copies, waits for them, and re-layouts  2.86 us

profile of v4, /device:TPU:2, one launch (start us, length us, event | category | flops | bytes accessed | tf_op | source)
XLA Modules:
  0.0 70.5 jit_solution(7463901527943083765)
XLA Ops:
  0.7 0.7 convert_element_type.3
  1.3 0.7 %pad_maximum_fusion = f32[640]{0:T(1024)S(1)} fusion(f32[123]{0:T(128)S(1)} %broadcast_in_dim.3, f32[1]{0:T(128)S(6)} %copy.7, f32[4]{0:T(128)} %param.9, f32[512]{0:T(512)S(1)} %convert_element_type.3), kind=kLoop, calls=%fused_computation | loop fusion | flops 1920 | bytes 5120 | tf_op jit(solution)/shard_map/concatenate | solution.py:524
  2.1 0.0 copy-start
  2.1 0.8 %copy-done = s32[8,16,16]{2,1,0:T(8,128)S(1)} copy-done((s32[8,16,16]{2,1,0:T(8,128)S(1)}, s32[8,16,16]{2,1,0:T(8,128)}, u32[]{:S(2)}) %copy-start) | copy-done | bytes 8216
  2.9 65.6 %shard_map.55 = f32[8,16,16,512]{3,2,1,0:T(8,128)S(1)} custom-call(f32[8,16,16,512]{3,2,1,0:T(8,128)} %dist.1, f32[1,640]{1,0:T(1,128)S(1)} %reshape.3.scalars_in, s32[8,16,16]{2,1,0:T(8,128)S(1)} %copy-done), custom_call_target="tpu_custom_call" | custom-call | tf_op jit(solution)/shard_map/pallas_call | solution.py:534
  68.5 2.0 %copy.8 = f32[8,16,16,512]{3,2,1,0:T(8,128)} copy(f32[8,16,16,512]{3,2,1,0:T(8,128)S(1)} %shard_map.55) | data formatting | bytes 8388608
  (2 shorter events, 0.0 us)
Async XLA Ops:
  2.1 0.8 %copy-start = (s32[8,16,16]{2,1,0:T(8,128)S(1)}, s32[8,16,16]{2,1,0:T(8,128)}, u32[]{:S(2)}) copy-start(s32[8,16,16]{2,1,0:T(8,128)} %codes_in.1) | copy-start | bytes 24580

commit v5 on v2

--- a/solution.py
+++ b/solution.py
@@ -249,14 +249,18 @@
 
         lax.fori_loop(0, (yc // yu) * tiles, tile, 0)
 
-    def block_moments(x, c):
-        flat = moved[x, pl.ds(c * yc, yc)].reshape(LANES, width)
+    def block_moments(places):
+        flat = jnp.concatenate(
+            [moved[x, pl.ds(c * yc, yc)].reshape(LANES, width) for x, c in places], axis=0
+        )
         high = flat.astype(jnp.bfloat16)
         low = (flat - high.astype(jnp.float32)).astype(jnp.bfloat16)
-        sums = jnp.dot(high, feat[...], preferred_element_type=jnp.float32) + jnp.dot(
-            low, feat[...], preferred_element_type=jnp.float32
-        )
-        return sums.T[0:8]
+        sums = jnp.dot(
+            jnp.concatenate([high, low], axis=0), feat[...], preferred_element_type=jnp.float32
+        )
+        count = len(places) * LANES
+        sums = sums[:count] + sums[count:]
+        return [sums[k * LANES:(k + 1) * LANES].T[0:8] for k in range(len(places))]
 
     def outer_copy(t, c, p):
         return pltpu.make_async_remote_copy(
@@ -280,14 +284,14 @@
 
     def moments_outer(t, c):
         for i, x in enumerate(outer_layers):
-            mom_outer[t, mv, c, i] = block_moments(x, c)
+            mom_outer[t, mv, c, i] = block_moments([(x, c)])[0]
         for p in range(1, nv):
             outer_copy(t, c, p).start()
 
     def moments_inner(t):
         def layer(i, _):
-            for c in range(chunks):
-                mom_inner[t, mv, i * chunks + c] = block_moments(i + 2, c)
+            for c, sums in enumerate(block_moments([(i + 2, c) for c in range(chunks)])):
+                mom_inner[t, mv, i * chunks + c] = sums
             return 0
 
         lax.fori_loop(0, inner_rows, layer, 0)
@@ -408,6 +412,7 @@
             yz(now, lambda i: i + 2 + split, inner_rows - split)
             x_inner(now)
             moments_inner(t)
+            fill_late()
 
         def fill_late():
             relax_inner(t, then)
@@ -427,9 +432,6 @@
             moments_outer(t, c)
             if c == 0:
                 fill_early()
-            if c == chunks - 1:
-                fill_late()
-
             @pl.when(last)
             def _():
                 if c == chunks - 1:

time: 68.3 us -> 83.6 us (1.22)
  Pallas kernels: 63.3 us -> 78.6 us
    pallas_call x1, Pallas kernels: 63.3 us -> 78.6 us  [body(): pl.pallas_call(functools.partial(kernel, rows, ny, nz, width, nx_dev, nv)...]
where the time goes in v5:
time: 83.6 us; the launch traced here: 83.4 us
  Pallas kernels  78.6 us (94%)
  local copies, waits for them, and re-layouts  4.18 us (5%)
    pallas_call x1, Pallas kernels, body(): pl.pallas_call(functools.partial(kernel, rows, ny, nz, width, nx_dev, nv)...  78.6 us
    unnamed x7, local copies, waits for them, and re-layouts  4.18 us

profile of v5, /device:TPU:2, one launch (start us, length us, event | category | flops | bytes accessed | tf_op | source)
XLA Modules:
  0.0 83.4 jit_solution(2771062209365546327)
XLA Ops:
  0.7 0.0 copy-start
  0.7 0.8 copy-done
  1.5 0.0 copy-start.1
  1.5 0.7 copy-done.1
  2.2 0.0 copy-start.2
  2.2 0.7 copy-done.2
  2.8 78.6 %shard_map.55 = f32[8,16,16,512]{3,2,1,0:T(8,128)S(1)} custom-call(f32[8,16,16,512]{3,2,1,0:T(8,128)} %dist.1, s32[1,512]{1,0:T(1,128)S(1)} %bitcast.4, s32[8,16,16]{2,1,0:T(8,128)S(1)} %copy-done, f32[1,1]{1,0:T(1,128)} %bitcast.3.knudsen_in, f32[1,4]{1,0:T(1,128)S(1)} %bitcast.5), custom_call_target="tpu_custom_call" | custom-call | tf_op jit(solution)/shard_map/pallas_call | solution.py:490
  81.4 2.0 %copy.8 = f32[8,16,16,512]{3,2,1,0:T(8,128)} copy(f32[8,16,16,512]{3,2,1,0:T(8,128)S(1)} %shard_map.55) | data formatting | bytes 8388608
Async XLA Ops:
  0.7 0.8 %copy-start = (s32[8,16,16]{2,1,0:T(8,128)S(1)}, s32[8,16,16]{2,1,0:T(8,128)}, u32[]{:S(2)}) copy-start(s32[8,16,16]{2,1,0:T(8,128)} %codes_in.1) | copy-start | bytes 24580
  1.5 0.7 copy-start.1
  2.2 0.7 copy-start.2

commit v6 on v2

--- a/solution.py
+++ b/solution.py
@@ -399,22 +399,7 @@
         then = 1 - now
         current = state.at[now]
         following = state.at[then]
-        split = inner_rows // 2
-
-        def fill_early():
-            yz(now, lambda i: i + 2, split)
-
-        def fill_between():
-            yz(now, lambda i: i + 2 + split, inner_rows - split)
-            x_inner(now)
-            moments_inner(t)
-
-        def fill_late():
-            relax_inner(t, then)
-
-        yz(now, outer_layer, 4)
-        for c in range(chunks):
-
+        def arrive(c):
             @pl.when(has_high)
             def _():
                 to_low(t, c, current).wait_recv()
@@ -425,16 +410,8 @@
 
             x_outer(t, now, c)
             moments_outer(t, c)
-            if c == 0:
-                fill_early()
-            if c == chunks - 1:
-                fill_late()
-
-            @pl.when(last)
-            def _():
-                if c == chunks - 1:
-                    write_inner().start()
-
+
+        def leave(c):
             relax_outer(t, then, c)
 
             @pl.when(jnp.logical_and(has_low, jnp.logical_not(last)))
@@ -450,8 +427,22 @@
                 for side in range(2):
                     write_outer(c, side).start()
 
-            if c == 0:
-                fill_between()
+        yz(now, outer_layer, 4)
+        for c in range(chunks - 1):
+            arrive(c)
+        yz(now, lambda i: i + 2, inner_rows)
+        x_inner(now)
+        moments_inner(t)
+        arrive(chunks - 1)
+        for c in range(chunks - 1):
+            leave(c)
+        relax_inner(t, then)
+
+        @pl.when(last)
+        def _():
+            write_inner().start()
+
+        leave(chunks - 1)
 
         for c in range(chunks):
 

time: 68.3 us -> 61 us (0.89); the launches traced: 68.2 us -> 59.9 us
  Pallas kernels: 63.3 us -> 55.1 us
    pallas_call x1, Pallas kernels: 63.3 us -> 55.1 us  [body(): pl.pallas_call(functools.partial(kernel, rows, ny, nz, width, nx_dev, nv)...]
where the time goes in v6:
time: 61 us; the launch traced here: 59.9 us
  Pallas kernels  55.1 us (90%)
  local copies, waits for them, and re-layouts  4.18 us (7%)
  between operations  0.67 us (1%)
    pallas_call x1, Pallas kernels, body(): pl.pallas_call(functools.partial(kernel, rows, ny, nz, width, nx_dev, nv)...  55.1 us
    unnamed x7, local copies, waits for them, and re-layouts  4.18 us

profile of v6, /device:TPU:2, one launch (start us, length us, event | category | flops | bytes accessed | tf_op | source)
XLA Modules:
  0.0 59.9 jit_solution(768675255352165003)
XLA Ops:
  0.7 0.0 copy-start
  0.7 0.8 %copy-done = s32[8,16,16]{2,1,0:T(8,128)S(1)} copy-done((s32[8,16,16]{2,1,0:T(8,128)S(1)}, s32[8,16,16]{2,1,0:T(8,128)}, u32[]{:S(2)}) %copy-start) | copy-done | bytes 8216
  1.5 0.0 copy-start.1
  1.5 0.7 %copy-done.1 = s32[512]{0:T(512)S(1)} copy-done((s32[512]{0:T(512)S(1)}, s32[512]{0:T(512)}, u32[]{:S(2)}) %copy-start.1) | copy-done | bytes 2072
  2.2 0.0 copy-start.2
  2.2 0.7 %copy-done.2 = f32[4]{0:T(128)S(1)} copy-done((f32[4]{0:T(128)S(1)}, f32[4]{0:T(128)}, u32[]{:S(2)}) %copy-start.2) | copy-done | bytes 40
  2.8 55.1 %shard_map.55 = f32[8,16,16,512]{3,2,1,0:T(8,128)S(1)} custom-call(f32[8,16,16,512]{3,2,1,0:T(8,128)} %dist.1, s32[1,512]{1,0:T(1,128)S(1)} %bitcast.4, s32[8,16,16]{2,1,0:T(8,128)S(1)} %copy-done, f32[1,1]{1,0:T(1,128)} %bitcast.3.knudsen_in, f32[1,4]{1,0:T(1,128)S(1)} %bitcast.5), custom_call_target="tpu_custom_call" | custom-call | tf_op jit(solution)/shard_map/pallas_call | solution.py:479
  57.9 2.0 %copy.8 = f32[8,16,16,512]{3,2,1,0:T(8,128)} copy(f32[8,16,16,512]{3,2,1,0:T(8,128)S(1)} %shard_map.55) | data formatting | bytes 8388608
Async XLA Ops:
  0.7 0.8 %copy-start = (s32[8,16,16]{2,1,0:T(8,128)S(1)}, s32[8,16,16]{2,1,0:T(8,128)}, u32[]{:S(2)}) copy-start(s32[8,16,16]{2,1,0:T(8,128)} %codes_in.1) | copy-start | bytes 24580
  1.5 0.7 %copy-start.1 = (s32[512]{0:T(512)S(1)}, s32[512]{0:T(512)}, u32[]{:S(2)}) copy-start(s32[512]{0:T(512)} %param.6) | copy-start | bytes 6148
  2.2 0.7 %copy-start.2 = (f32[4]{0:T(128)S(1)}, f32[4]{0:T(128)}, u32[]{:S(2)}) copy-start(f32[4]{0:T(128)} %param.9) | copy-start | bytes 52
